TPU v7x, 32 devices: a whole 2x2x4 slice. The times are simulated.
32 devices in a mesh: sens: 8 (over y, x, core), grp: 4 (over z).
Axes of the slice: x: 2, y: 2, z: 4, core: 2. Of those that a mesh axis runs over, the one named last changes fastest.
Arguments:
- histories: bfloat16 [256, 4096], P('sens', 'grp'), may hold values from -6 to 6
- bin_index: int32 [16], replicated, may hold values from 1 to 2047
- delays: int32 [256, 4096], P('sens'), may hold values from 0 to 4095
- map_adjoint: float32 [4096], replicated, may hold values from -48 to 48
Outputs:
- history_adjoint: bfloat16 [256, 4096], P('sens', 'grp')
Inputs may be any that keep to these rules, and one draw needn't show every extreme that they name: `delays`: each delay is already reduced modulo 4096.
All inputs are finite; a program needn't handle non-finite values.
Results may differ from a plain program's by a relative error of at most 0.0059.
Values may be sent and summed in bfloat16 or wider, within the bound.
A program may use at most 64 MiB of HBM per device.

v0:
```python
import math

import jax
import jax.numpy as jnp
from jax import lax
from jax.sharding import PartitionSpec as P

NT = 4096


two_pi = 2.0 * math.pi


def grouped_transform(first_sample, sample_count, bin_index, length, groups):
    sample_times = first_sample + lax.iota(jnp.int32, sample_count)
    phase_index = sample_times[:, None] * bin_index[None, :] % length
    phase_angle = phase_index.astype(jnp.float32) * (two_pi / length)
    factor = 1.0 / math.sqrt(length)
    bin_width = bin_index.shape[0] // groups
    cosine = (jnp.cos(phase_angle) * factor).reshape(sample_count, groups, 1, bin_width)
    sine_part = (-jnp.sin(phase_angle) * factor).reshape(sample_count, groups, 1, bin_width)
    joined_parts = jnp.concatenate([cosine, sine_part], 2)
    return joined_parts.reshape(sample_count, 2 * bin_index.shape[0]).astype(jnp.bfloat16)


def angles(bin_index, delay_block, length):
    phase_index = bin_index[:, None, None] * delay_block[None, :, :] % length
    return phase_index.astype(jnp.float32) * (two_pi / length)


def steer_forward(real_part, imag_part, delays, bin_index, length, steer_scale):
    scan_count = delays.shape[1]
    block_size = math.gcd(scan_count, 512)
    real_trans = real_part.T
    imag_trans = imag_part.T
    highest = lax.Precision.HIGHEST

    def one_block(block_index):
        delay_block = lax.dynamic_slice_in_dim(delays, block_index * block_size, block_size, 1)
        phase_angle = angles(bin_index, delay_block, length)
        cosine = jnp.cos(phase_angle)
        sine_part = jnp.sin(phase_angle)
        steer_real = jnp.einsum("fs,fsg->fg", real_trans, cosine, precision=highest) - jnp.einsum(
            "fs,fsg->fg", imag_trans, sine_part, precision=highest
        )
        steer_imag = jnp.einsum(
            "fs,fsg->fg", real_trans, sine_part, precision=highest
        ) + jnp.einsum("fs,fsg->fg", imag_trans, cosine, precision=highest)
        return (steer_real * steer_scale, steer_imag * steer_scale)

    blocks_real, blocks_imag = lax.map(
        one_block, jnp.arange(scan_count // block_size, dtype=jnp.int32)
    )
    bin_count = bin_index.shape[0]
    return (
        blocks_real.transpose(1, 0, 2).reshape(bin_count, scan_count),
        blocks_imag.transpose(1, 0, 2).reshape(bin_count, scan_count),
    )


def steer_back(bar_real, bar_imag, delays, bin_index, length, steer_scale):
    scan_count = delays.shape[1]
    block_size = math.gcd(scan_count, 512)
    highest = lax.Precision.HIGHEST

    def add_block(block_index, totals):
        delay_block = lax.dynamic_slice_in_dim(delays, block_index * block_size, block_size, 1)
        block_real = lax.dynamic_slice_in_dim(bar_real, block_index * block_size, block_size, 1)
        block_imag = lax.dynamic_slice_in_dim(bar_imag, block_index * block_size, block_size, 1)
        phase_angle = angles(bin_index, delay_block, length)
        cosine = jnp.cos(phase_angle)
        sine_part = jnp.sin(phase_angle)
        back_real = jnp.einsum("fg,fsg->fs", block_real, cosine, precision=highest) + jnp.einsum(
            "fg,fsg->fs", block_imag, sine_part, precision=highest
        )
        back_imag = jnp.einsum("fg,fsg->fs", block_imag, cosine, precision=highest) - jnp.einsum(
            "fg,fsg->fs", block_real, sine_part, precision=highest
        )
        return (totals[0] + back_real, totals[1] + back_imag)

    zeros_start = jnp.zeros((bin_index.shape[0], delays.shape[0]), jnp.float32)
    total_real, total_imag = lax.fori_loop(
        0, scan_count // block_size, add_block, (zeros_start, zeros_start)
    )
    return (total_real.T * steer_scale, total_imag.T * steer_scale)


def on_device(histories, bin_index, delays, map_adjoint):
    groups = lax.axis_size("grp")
    sensors = delays.shape[0] * lax.axis_size("sens")
    steer_scale = 1.0 / math.sqrt(sensors)
    block_rows = histories.shape[1]
    position = lax.axis_index("grp")
    weight = 2.0 * map_adjoint[None, :]
    transform = grouped_transform(position * block_rows, block_rows, bin_index, NT, groups)
    partial_value = jnp.dot(histories, transform, preferred_element_type=jnp.float32)
    spectra = lax.psum_scatter(partial_value, "grp", scatter_dimension=1, tiled=True)
    bin_width = bin_index.shape[0] // groups
    own_bins = lax.dynamic_slice_in_dim(bin_index, position * bin_width, bin_width, 0)
    real_part = spectra[:, :bin_width]
    imag_part = spectra[:, bin_width:]
    steer_real, steer_imag = steer_forward(real_part, imag_part, delays, own_bins, NT, steer_scale)
    steer_real, steer_imag = lax.psum((steer_real, steer_imag), "sens")
    back_real, back_imag = steer_back(
        weight * steer_real, weight * steer_imag, delays, own_bins, NT, steer_scale
    )
    adjoint = jnp.concatenate([back_real, back_imag], 1).astype(jnp.bfloat16)
    result = lax.dot_general(
        lax.all_gather(adjoint, "grp", axis=1, tiled=True),
        transform,
        (((1,), (1,)), ((), ())),
        preferred_element_type=jnp.float32,
    )
    return result.astype(jnp.bfloat16)


def solution(mesh):
    placed = (P("sens", "grp"), P(), P("sens", None), P())
    return jax.shard_map(
        on_device, mesh=mesh, in_specs=placed, out_specs=P("sens", "grp"), check_vma=False
    )
```

profile of v0, /device:TPU:0, one launch (start us, length us, event | category | flops | bytes accessed | tf_op | source)
XLA Modules:
  0.0 216.6 jit_solution(2575019335760115923)
XLA Ops:
  8.2 20.5 %all-reduce = f32[32,32]{0,1:T(8,128)S(1)} all-reduce(f32[32,32]{0,1:T(8,128)S(1)} %convolution_bitcast_fusion), channel_id=2, replica_groups=mesh['sens'=8,'grp'=4] {'grp'}, use_global_device_ids=true, to_apply=%region_0.1.clone | all-reduce | flops 1024 | bytes 8192
  30.7 63.2 %while.32 = (s32[]{:T(128)}, f32[8,4,512]{2,1,0:T(4,128)}, f32[8,4,512]{2,1,0:T(4,128)}, s32[4]{0:T(128)S(1)}, s32[8]{0:T(128)S(1)}, /*index=5*/s32[32,4096]{1,0...) while((s32[]{:T(128)}, f32[8,4,512]{2,1,0:T(4,128)}, ...), condition=%wide.region_2.3_spmd, body=%wide.region_1.2_spmd.sunk | while | flops 6823942 | bytes 477939 | solution.py:51
  94.6 50.7 %all-reduce.4.cloned.1.call-done = (f32[4,4096]{1,0:T(4,128)}, f32[4,4096]{1,0:T(4,128)}) async-done(((f32[4,4096]{1,0:T(4,128)}, f32[4,4096]{1,0:T(4,128)}), (f32[4,4096]{1,0:T(4,128)}, f32[4,4096]{1,0:T(4,128)})) %all-reduce.4.cloned.1.call-update) | async-done | bytes 131088 | tf_op jit(solution)/shard_map/psum | solution.py:103
  146.2 50.8 %while.33 = (s32[]{:T(128)}, f32[4,32]{1,0:T(4,128)S(1)}, f32[4,32]{1,0:T(4,128)S(1)}, f32[4,4096]{1,0:T(4,128)S(1)}, s32[4]{0:T(128)S(1)}, /*index=5*/s32[32,40...) while((s32[]{:T(128)}, f32[4,32]{1,0:T(4,128)S(1)}, ...), condition=%wide.region_6.7_spmd.clone, body=%wide.region_5.6_spmd.clone.sunk | while | flops 6816519 | bytes 465134 | solution.py:82
  147.1 1.3 fusion.123
  148.4 1.4 fusion.124
  149.8 1.4 fusion.122
  151.2 1.4 fusion.121
  154.8 1.4 fusion.124
  156.1 1.4 fusion.122
  157.5 1.4 fusion.121
  159.8 1.3 fusion.123
  161.1 1.4 fusion.124
  162.5 1.4 fusion.122
  163.9 1.4 fusion.121
  167.5 1.4 fusion.124
  168.8 1.4 fusion.122
  170.2 1.4 fusion.121
  173.8 1.4 fusion.124
  175.2 1.4 fusion.122
  176.6 1.4 fusion.121
  178.8 1.3 fusion.123
  180.2 1.4 fusion.124
  181.6 1.4 fusion.122
  182.9 1.4 fusion.121
  186.5 1.4 fusion.124
  187.9 1.4 fusion.122
  189.3 1.4 fusion.121
  192.9 1.4 fusion.124
  194.3 1.4 fusion.122
  195.6 1.4 fusion.121
  197.1 11.9 %all_gather.3 = bf16[32,32]{0,1:T(8,128)(2,1)S(1)} all-gather(bf16[32,8]{0,1:T(8,128)(2,1)S(1)} %pad_maximum_fusion.1), channel_id=1, replica_groups=mesh['sens'=8,'grp'=4] {'grp'}, dimensions={1}, use_global_device_ids=true | all-gather | bytes 2560 | tf_op jit(solution)/shard_map/all_gather | solution.py:109
  (123 shorter events, 76.9 us)
Async XLA Ops:
  6.5 1.6 copy-start
  6.5 138.8 %all-reduce.4.cloned.1.call-start = ((), (), s32[]{:S(2)}) async-start(), calls=%async_computation | async-start | bytes 262144 | tf_op jit(solution)/shard_map/psum | solution.py:103
  6.5 0.7 copy-start.2
  28.7 0.7 copy-start.3
  93.9 0.7 copy-start.1
Sparse Core Ops, SparseCore 0:
  94.0 51.2 all-reduce.3
where the time goes:
time: 218 us; the launch traced here: 217 us
  matrix products  85.7 us (39%)
  waiting for transfers between devices  50.7 us (23%)
  blocking collectives  32.4 us (15%)
  local copies, waits for them, and re-layouts  21.3 us (10%)
  between operations  14.1 us (6%)
  other arithmetic  6.74 us (3%)
  loops' own time  5.65 us (3%)
    psum x1, waiting for transfers between devices, on_device(): steer_real, steer_imag = lax.psum((steer_real, steer_imag), 'sens')  50.7 us
    unnamed x1, blocking collectives  20.5 us
    all_gather x1, blocking collectives, on_device(): lax.all_gather(adjoint, 'grp', axis=1, tiled=True)  11.9 us
    dot_general x8, matrix products, add_block(): jnp.einsum('fg,fsg->fs', block_real, sine_part, precision=highest)  11 us
    dot_general x8, matrix products, add_block(): jnp.einsum('fg,fsg->fs', block_imag, sine_part, precision=highest)  11 us
    dot_general x8, matrix products, add_block(): jnp.einsum('fg,fsg->fs', block_real, cosine, precision=highest)  10.9 us
    dot_general x8, matrix products, add_block(): jnp.einsum('fg,fsg->fs', block_imag, cosine, precision=highest)  10.7 us
    dot_general x8, matrix products, one_block(): jnp.einsum('fs,fsg->fg', real_trans, sine_part, precision=highest)  10.3 us
  transfers between devices with their start and end apart: 1, of which 1 were waited for; matrix products, arithmetic and copies ran while one was open for 0% of the time, Pallas kernels for 0%

commit v1 on v0

--- a/solution.py
+++ b/solution.py
@@ -1,8 +1,11 @@
+import functools
 import math
 
 import jax
 import jax.numpy as jnp
 from jax import lax
+from jax.experimental import pallas as pl
+from jax.experimental.pallas import tpu as pltpu
 from jax.sharding import PartitionSpec as P
 
 NT = 4096
@@ -85,7 +88,7 @@
     return (total_real.T * steer_scale, total_imag.T * steer_scale)
 
 
-def on_device(histories, bin_index, delays, map_adjoint):
+def on_device_plain(histories, bin_index, delays, map_adjoint):
     groups = lax.axis_size("grp")
     sensors = delays.shape[0] * lax.axis_size("sens")
     steer_scale = 1.0 / math.sqrt(sensors)
@@ -114,8 +117,304 @@
     return result.astype(jnp.bfloat16)
 
 
+MESH = pl.DeviceIdType.MESH
+COS_T = (0.9999992216, -19.73898252, 64.92872662, -85.27239701, 58.79403871, -21.07678212)
+SIN_T = (6.283055799, -41.33121431, 81.36681529, -74.47800454, 32.78140079)
+COS_W = (
+    0.9999999892,
+    -19.73920453,
+    64.93911898,
+    -85.45016555,
+    60.16783172,
+    -25.96831327,
+    6.529610372,
+)
+CHUNK = 256
+
+
+def horner(coefficients, u):
+    value = coefficients[-1] * u + coefficients[-2]
+    for coefficient in coefficients[-3::-1]:
+        value = value * u + coefficient
+    return value
+
+
+def wrapped(turns):
+    return turns - jnp.round(turns)
+
+
+def kernel(
+    ns,
+    ng,
+    scale,
+    bins_ref,
+    map_ref,
+    hist_hbm,
+    delays_hbm,
+    out_ref,
+    hist,
+    delays,
+    wave,
+    steer,
+    spec_out,
+    spec_in,
+    part_out,
+    part_in,
+    bar_out,
+    bar_in,
+    adj,
+    local_sem,
+    spec_send,
+    spec_recv,
+    part_send,
+    part_recv,
+    bar_send,
+    bar_recv,
+    adj_send,
+    adj_recv,
+):
+    f32, bf16 = jnp.float32, jnp.bfloat16
+    sens, grp = lax.axis_index("sens"), lax.axis_index("grp")
+    rows, times = hist.shape
+    points = delays.shape[1]
+    width = points // ns
+    half = width // 2
+    blocks = wave.shape[0] // 16
+    length = times * ng
+
+    def sens_at(offset):
+        return lax.rem(sens + offset, ns)
+
+    def grp_at(offset):
+        return lax.rem(grp + offset, ng)
+
+    hist_copy = pltpu.make_async_copy(hist_hbm, hist, local_sem.at[0])
+    delays_copy = pltpu.make_async_copy(delays_hbm, delays, local_sem.at[1])
+    hist_copy.start()
+    delays_copy.start()
+    barrier = pltpu.get_barrier_semaphore()
+    for k in range(1, ns):
+        pl.semaphore_signal(barrier, inc=1, device_id={"sens": sens_at(k)}, device_id_type=MESH)
+    for k in range(1, ng):
+        pl.semaphore_signal(barrier, inc=1, device_id={"grp": grp_at(k)}, device_id_type=MESH)
+
+    row8 = lax.broadcasted_iota(jnp.int32, (8, times), 0)
+    sample = (grp * times + lax.broadcasted_iota(jnp.int32, (8, times), 1)).astype(f32)
+    lower = row8 >= 4
+    which = lax.rem(row8, 4)
+    for j in range(blocks):
+        b = [bins_ref[4 * j + i].astype(f32) * (1.0 / length) for i in range(4)]
+        column = jnp.where(
+            which == 0, b[0], jnp.where(which == 1, b[1], jnp.where(which == 2, b[2], b[3]))
+        )
+        r = wrapped(sample * column + jnp.where(lower, 0.25, 0.0))
+        values = horner(COS_W, r * r) * (1.0 / math.sqrt(length))
+        wave[16 * j : 16 * j + 16, :] = jnp.concatenate(
+            [values, jnp.zeros((8, times), f32)], 0
+        ).astype(bf16)
+
+    hist_copy.wait()
+    partial_spectra = lax.dot_general(
+        wave[...], hist[...], (((1,), (1,)), ((), ())), preferred_element_type=f32
+    )
+    spec_out[...] = jnp.zeros(spec_out.shape, f32)
+    for j in range(ng):
+        spec_out[j, :, 0:rows] = partial_spectra[16 * j : 16 * j + 8, :]
+    pl.semaphore_wait(barrier, ns - 1 + ng - 1)
+
+    spec_copies = []
+    for k in range(1, ng):
+        copy = pltpu.make_async_remote_copy(
+            src_ref=spec_out.at[grp_at(k)],
+            dst_ref=spec_in.at[k - 1],
+            send_sem=spec_send.at[k - 1],
+            recv_sem=spec_recv.at[k - 1],
+            device_id={"grp": grp_at(k)},
+            device_id_type=MESH,
+        )
+        copy.start()
+        spec_copies.append(copy)
+
+    delays_copy.wait()
+    own_bins = [bins_ref[4 * grp + i].astype(f32) * (1.0 / length) for i in range(4)]
+
+    def steer_chunk(index, carry):
+        at = pl.ds(pl.multiple_of(index * CHUNK, CHUNK), CHUNK)
+        delay = delays[:, at].astype(f32)
+        for i in range(4):
+            r = wrapped(delay * own_bins[i])
+            u = r * r
+            steer[64 * i : 64 * i + 32, at] = horner(COS_T, u).astype(bf16)
+            steer[64 * i + 32 : 64 * i + 64, at] = (horner(SIN_T, u) * r).astype(bf16)
+        return carry
+
+    lax.fori_loop(0, points // CHUNK, steer_chunk, 0)
+
+    sign = jnp.where(lax.broadcasted_iota(jnp.int32, (8, 128), 0) < 4, -1.0, 1.0).astype(f32)
+    own_block = lax.rem(lax.broadcasted_iota(jnp.int32, (8, 256), 0), 4) == (
+        lax.broadcasted_iota(jnp.int32, (8, 256), 1) // 64
+    )
+    total = spec_out[grp]
+    for k in range(1, ng):
+        spec_copies[k - 1].wait_recv()
+        total = total + spec_in[k - 1]
+    both = total + pltpu.roll(sign * pltpu.roll(total, 4, 0), 32, 1)
+    both = both + pltpu.roll(both, 64, 1)
+    spread = jnp.where(own_block, jnp.concatenate([both, both], 1), 0.0)
+    high = spread.astype(bf16).astype(f32)
+    lhs = jnp.concatenate([high, spread - high], 0).astype(bf16)
+
+    def steered_part(owner):
+        at = pl.ds(pl.multiple_of(owner * width, width), width)
+        product = jnp.dot(lhs, steer[:, at], preferred_element_type=f32)
+        product = product[0:8] + product[8:16]
+        return jnp.concatenate([product[:, 0:half], product[:, half:width]], 0)
+
+    part_copies = []
+    for k in range(1, ns):
+        part_out[k - 1] = steered_part(sens_at(k)).astype(bf16)
+        copy = pltpu.make_async_remote_copy(
+            src_ref=part_out.at[k - 1],
+            dst_ref=part_in.at[k - 1],
+            send_sem=part_send.at[k - 1],
+            recv_sem=part_recv.at[k - 1],
+            device_id={"sens": sens_at(k)},
+            device_id_type=MESH,
+        )
+        copy.start()
+        part_copies.append(copy)
+    total = steered_part(sens)
+    first = map_ref[:, pl.ds(pl.multiple_of(sens * width, width), half)]
+    second = map_ref[:, pl.ds(pl.multiple_of(sens * width + half, half), half)]
+    weight = (2.0 * scale * scale) * jnp.concatenate(
+        [jnp.broadcast_to(first, (8, half)), jnp.broadcast_to(second, (8, half))], 0
+    )
+    for k in range(1, ns):
+        part_copies[k - 1].wait_recv()
+        total = total + part_in[k - 1].astype(f32)
+    bar = (weight * total).astype(bf16)
+    bar_out[...] = bar
+
+    bar_copies = []
+    for k in range(1, ns):
+        copy = pltpu.make_async_remote_copy(
+            src_ref=bar_out,
+            dst_ref=bar_in.at[k - 1],
+            send_sem=bar_send.at[k - 1],
+            recv_sem=bar_recv.at[k - 1],
+            device_id={"sens": sens_at(k)},
+            device_id_type=MESH,
+        )
+        copy.start()
+        bar_copies.append(copy)
+
+    def back_part(values, owner):
+        sides = []
+        for side in range(2):
+            at = pl.ds(pl.multiple_of(owner * width + side * half, half), half)
+            sides.append(
+                lax.dot_general(
+                    values,
+                    steer[:, at],
+                    (((1,), (1,)), ((), ())),
+                    preferred_element_type=f32,
+                )
+            )
+        return sides[0][0:8] + sides[1][8:16]
+
+    back = back_part(bar, sens)
+    for k in range(1, ns):
+        bar_copies[k - 1].wait_recv()
+        back = back + back_part(bar_in[k - 1], sens_at(ns - k))
+    back = jnp.where(own_block, back, 0.0)
+    back = back[:, 0:128] + back[:, 128:256]
+    back = back + pltpu.roll(back, 64, 1)
+    back = back - sign * pltpu.roll(pltpu.roll(back, 4, 0), 96, 1)
+    own_rows = jnp.concatenate([back, jnp.zeros((8, 128), f32)], 0).astype(bf16)
+    adj[grp] = own_rows
+
+    adj_copies = []
+    for k in range(1, ng):
+        copy = pltpu.make_async_remote_copy(
+            src_ref=adj.at[grp],
+            dst_ref=adj.at[grp],
+            send_sem=adj_send.at[k - 1],
+            recv_sem=adj_recv.at[k - 1],
+            device_id={"grp": grp_at(k)},
+            device_id_type=MESH,
+        )
+        copy.start()
+        adj_copies.append(copy)
+    for copy in adj_copies:
+        copy.wait_recv()
+    gathered = jnp.concatenate([adj[j] for j in range(ng)], 0)
+    out_ref[...] = lax.dot_general(
+        gathered[:, 0:rows], wave[...], (((0,), (0,)), ((), ())), preferred_element_type=f32
+    ).astype(bf16)
+    for copy in spec_copies + part_copies + bar_copies + adj_copies:
+        copy.wait_send()
+
+
+def on_device_fused(ns, ng, histories, bin_index, delays, map_adjoint):
+    rows, times = histories.shape
+    points = delays.shape[1]
+    half = points // ns // 2
+    dma = pltpu.SemaphoreType.DMA
+    vmem = pltpu.VMEM
+    return pl.pallas_call(
+        functools.partial(kernel, ns, ng, 1.0 / math.sqrt(rows * ns)),
+        out_shape=jax.ShapeDtypeStruct((rows, times), jnp.bfloat16),
+        in_specs=[
+            pl.BlockSpec(memory_space=pltpu.SMEM),
+            pl.BlockSpec(memory_space=pltpu.VMEM),
+            pl.BlockSpec(memory_space=pl.ANY),
+            pl.BlockSpec(memory_space=pl.ANY),
+        ],
+        out_specs=pl.BlockSpec(memory_space=pltpu.VMEM),
+        scratch_shapes=[
+            vmem((rows, times), jnp.bfloat16),
+            vmem((rows, points), jnp.int32),
+            vmem((16 * ng, times), jnp.bfloat16),
+            vmem((256, points), jnp.bfloat16),
+            vmem((ng, 8, 128), jnp.float32),
+            vmem((ng - 1, 8, 128), jnp.float32),
+            vmem((ns - 1, 16, half), jnp.bfloat16),
+            vmem((ns - 1, 16, half), jnp.bfloat16),
+            vmem((16, half), jnp.bfloat16),
+            vmem((ns - 1, 16, half), jnp.bfloat16),
+            vmem((ng, 16, 128), jnp.bfloat16),
+            dma((2,)),
+            dma((ng - 1,)),
+            dma((ng - 1,)),
+            dma((ns - 1,)),
+            dma((ns - 1,)),
+            dma((ns - 1,)),
+            dma((ns - 1,)),
+            dma((ng - 1,)),
+            dma((ng - 1,)),
+        ],
+        compiler_params=pltpu.CompilerParams(
+            collective_id=0, has_side_effects=True, vmem_limit_bytes=32 * 1024 * 1024
+        ),
+    )(bin_index, map_adjoint.reshape(1, points), histories, delays)
+
+
 def solution(mesh):
+    ns, ng = mesh.shape["sens"], mesh.shape["grp"]
     placed = (P("sens", "grp"), P(), P("sens", None), P())
+
+    def on_device(histories, bin_index, delays, map_adjoint):
+        rows, points = delays.shape
+        fits = (
+            rows == 32
+            and bin_index.shape[0] == 4 * ng
+            and points % (256 * ns) == 0
+            and histories.shape[1] * ng == NT
+        )
+        if fits:
+            return on_device_fused(ns, ng, histories, bin_index, delays, map_adjoint)
+        return on_device_plain(histories, bin_index, delays, map_adjoint)
+
     return jax.shard_map(
         on_device, mesh=mesh, in_specs=placed, out_specs=P("sens", "grp"), check_vma=False
     )

time: 218 us -> 26.2 us (0.12)
  matrix products: 85.7 us -> 0 us
  waiting for transfers between devices: 50.7 us -> 0 us
  blocking collectives: 32.4 us -> 0 us
  Pallas kernels: 0 us -> 22 us
  local copies, waits for them, and re-layouts: 21.3 us -> 3.88 us
  between operations: 14.1 us -> 0.01 us
  other arithmetic: 6.74 us -> 0 us
  loops' own time: 5.65 us -> 0 us
    dot_general x66 -> x0, matrix products: 85.7 us -> none  [the longest x8 11 us: add_block(): jnp.einsum('fg,fsg->fs', block_real, sine_part, precision=highest)]
    psum x1 -> x0, waiting for transfers between devices: 50.7 us -> none  [on_device(): steer_real, steer_imag = lax.psum((steer_real, steer_imag), 'sens')]
    pallas_call x0 -> x1, Pallas kernels: none -> 22 us  [on_device_fused(): pl.pallas_call(functools.partial(kernel, ns, ng, 1.0 / math.sqrt(rows * n...]
    unnamed x1 -> x0, blocking collectives: 20.5 us -> none
    dynamic_slice x33 -> x0, local copies, waits for them, and re-layouts: 18.5 us -> none  [the longest x8 6.8 us: one_block(): lax.dynamic_slice_in_dim(delays, block_index * block_size, block_size, 1)]
    all_gather x1 -> x0, blocking collectives: 11.9 us -> none  [on_device(): lax.all_gather(adjoint, 'grp', axis=1, tiled=True)]
    another operation x2 -> x0, loops' own time: 5.65 us -> none  [the longest x1 5.42 us: steer_forward(): lax.map(one_block, jnp.arange(scan_count // block_size, dtype=jnp.int32))]
    dynamic_update_slice x8 -> x0, other arithmetic: 4.94 us -> none  [steer_forward(): lax.map(one_block, jnp.arange(scan_count // block_size, dtype=jnp.int32))]
  transfers between devices with their start and end apart: 1 -> 0, of which waited for: 1 -> 0; matrix products, arithmetic and copies ran while one was open for 0% -> 0% of each run, Pallas kernels for 0% -> 0%
where the time goes in v1:
time: 26.2 us; the launch traced here: 25.9 us
  Pallas kernels  22 us (84%)
  local copies, waits for them, and re-layouts  3.88 us (15%)
    pallas_call x1, Pallas kernels, on_device_fused(): pl.pallas_call(functools.partial(kernel, ns, ng, 1.0 / math.sqrt(rows * n...  22 us
    unnamed x9, local copies, waits for them, and re-layouts  3.88 us

profile of v1, /device:TPU:0, one launch (start us, length us, event | category | flops | bytes accessed | tf_op | source)
XLA Modules:
  0.0 25.9 jit_solution(1114650505430443989)
XLA Ops:
  0.0 0.0 copy-start.3
  0.0 0.7 %copy-done.3 = s32[16]{0:T(128)S(1)} copy-done((s32[16]{0:T(128)S(1)}, s32[16]{0:T(128)}, u32[]{:S(2)}) %copy-start.3) | copy-done | bytes 88
  0.7 0.0 copy-start
  0.7 1.0 %copy-done = s32[32,4096]{1,0:T(8,128)S(1)} copy-done((s32[32,4096]{1,0:T(8,128)S(1)}, s32[32,4096]{1,0:T(8,128)}, u32[]{:S(2)}) %copy-start) | copy-done | bytes 524312
  1.7 0.0 copy-start.1
  1.7 0.8 %copy-done.1 = bf16[32,1024]{1,0:T(8,128)(2,1)S(1)} copy-done((bf16[32,1024]{1,0:T(8,128)(2,1)S(1)}, bf16[32,1024]{1,0:T(8,128)(2,1)}, u32[]{:S(2)}) %copy-start.1) | copy-done | bytes 65560
  2.5 0.0 copy-start.2
  2.5 0.7 %copy-done.2 = f32[4096]{0:T(1024)S(1)} copy-done((f32[4096]{0:T(1024)S(1)}, f32[4096]{0:T(1024)}, u32[]{:S(2)}) %copy-start.2) | copy-done | bytes 16408
  3.3 22.0 %shard_map.46 = bf16[32,1024]{1,0:T(8,128)(2,1)S(1)} custom-call(s32[16]{0:T(128)S(1)} %copy-done.3, f32[1,4096]{1,0:T(1,128)S(1)} %bitcast.1, bf16[32,1024]{1,0:T(8,128)(2,1)S(1)} %copy-done.1, s32[32,4096]{1,0:T(8,128)S(1)} %copy-done), custom_call_target="tpu_custom_call" | custom-call | tf_op jit(solution)/shard_map/pallas_call | solution.py:364
  25.3 0.6 %copy.6 = bf16[32,1024]{1,0:T(8,128)(2,1)} copy(bf16[32,1024]{1,0:T(8,128)(2,1)S(1)} %shard_map.46) | data formatting | bytes 131072
Async XLA Ops:
  0.0 0.7 %copy-start.3 = (s32[16]{0:T(128)S(1)}, s32[16]{0:T(128)}, u32[]{:S(2)}) copy-start(s32[16]{0:T(128)} %bins_ref.1) | copy-start | bytes 196
  0.7 1.0 %copy-start = (s32[32,4096]{1,0:T(8,128)S(1)}, s32[32,4096]{1,0:T(8,128)}, u32[]{:S(2)}) copy-start(s32[32,4096]{1,0:T(8,128)} %delays_hbm.1) | copy-start | bytes 1572868
  1.7 0.8 %copy-start.1 = (bf16[32,1024]{1,0:T(8,128)(2,1)S(1)}, bf16[32,1024]{1,0:T(8,128)(2,1)}, u32[]{:S(2)}) copy-start(bf16[32,1024]{1,0:T(8,128)(2,1)} %hist_hbm.1) | copy-start | bytes 196612
  2.5 0.7 %copy-start.2 = (f32[4096]{0:T(1024)S(1)}, f32[4096]{0:T(1024)}, u32[]{:S(2)}) copy-start(f32[4096]{0:T(1024)} %param.7) | copy-start | bytes 49156

commit v2 on v1

--- a/solution.py
+++ b/solution.py
@@ -147,11 +147,13 @@
     ns,
     ng,
     scale,
-    bins_ref,
-    map_ref,
+    bins_hbm,
+    map_hbm,
     hist_hbm,
     delays_hbm,
     out_ref,
+    bins_ref,
+    map_own,
     hist,
     delays,
     wave,
@@ -190,8 +192,13 @@
 
     hist_copy = pltpu.make_async_copy(hist_hbm, hist, local_sem.at[0])
     delays_copy = pltpu.make_async_copy(delays_hbm, delays, local_sem.at[1])
+    bins_copy = pltpu.make_async_copy(bins_hbm, bins_ref, local_sem.at[2])
+    map_at = pl.ds(pl.multiple_of(sens * width, width), width)
+    map_copy = pltpu.make_async_copy(map_hbm.at[:, map_at], map_own, local_sem.at[3])
+    bins_copy.start()
     hist_copy.start()
     delays_copy.start()
+    map_copy.start()
     barrier = pltpu.get_barrier_semaphore()
     for k in range(1, ns):
         pl.semaphore_signal(barrier, inc=1, device_id={"sens": sens_at(k)}, device_id_type=MESH)
@@ -202,6 +209,7 @@
     sample = (grp * times + lax.broadcasted_iota(jnp.int32, (8, times), 1)).astype(f32)
     lower = row8 >= 4
     which = lax.rem(row8, 4)
+    bins_copy.wait()
     for j in range(blocks):
         b = [bins_ref[4 * j + i].astype(f32) * (1.0 / length) for i in range(4)]
         column = jnp.where(
@@ -284,8 +292,9 @@
         copy.start()
         part_copies.append(copy)
     total = steered_part(sens)
-    first = map_ref[:, pl.ds(pl.multiple_of(sens * width, width), half)]
-    second = map_ref[:, pl.ds(pl.multiple_of(sens * width + half, half), half)]
+    map_copy.wait()
+    first = map_own[:, 0:half]
+    second = map_own[:, half:width]
     weight = (2.0 * scale * scale) * jnp.concatenate(
         [jnp.broadcast_to(first, (8, half)), jnp.broadcast_to(second, (8, half))], 0
     )
@@ -365,13 +374,15 @@
         functools.partial(kernel, ns, ng, 1.0 / math.sqrt(rows * ns)),
         out_shape=jax.ShapeDtypeStruct((rows, times), jnp.bfloat16),
         in_specs=[
-            pl.BlockSpec(memory_space=pltpu.SMEM),
-            pl.BlockSpec(memory_space=pltpu.VMEM),
-            pl.BlockSpec(memory_space=pl.ANY),
-            pl.BlockSpec(memory_space=pl.ANY),
+            pl.BlockSpec(memory_space=pltpu.HBM),
+            pl.BlockSpec(memory_space=pltpu.HBM),
+            pl.BlockSpec(memory_space=pltpu.HBM),
+            pl.BlockSpec(memory_space=pltpu.HBM),
         ],
         out_specs=pl.BlockSpec(memory_space=pltpu.VMEM),
         scratch_shapes=[
+            pltpu.SMEM((bin_index.shape[0],), jnp.int32),
+            vmem((1, 2 * half), jnp.float32),
             vmem((rows, times), jnp.bfloat16),
             vmem((rows, points), jnp.int32),
             vmem((16 * ng, times), jnp.bfloat16),
@@ -383,7 +394,7 @@
             vmem((16, half), jnp.bfloat16),
             vmem((ns - 1, 16, half), jnp.bfloat16),
             vmem((ng, 16, 128), jnp.bfloat16),
-            dma((2,)),
+            dma((4,)),
             dma((ng - 1,)),
             dma((ng - 1,)),
             dma((ns - 1,)),
@@ -394,7 +405,7 @@
             dma((ng - 1,)),
         ],
         compiler_params=pltpu.CompilerParams(
-            collective_id=0, has_side_effects=True, vmem_limit_bytes=32 * 1024 * 1024
+            collective_id=0, has_side_effects=True, vmem_limit_bytes=64 * 1024 * 1024
         ),
     )(bin_index, map_adjoint.reshape(1, points), histories, delays)
 

time: 26.2 us -> 23.6 us (0.901)
  local copies, waits for them, and re-layouts: 3.88 us -> 1.47 us
    unnamed x9 -> x1, local copies, waits for them, and re-layouts: 3.88 us -> 1.47 us
where the time goes in v2:
time: 23.6 us; the launch traced here: 23.4 us
  Pallas kernels  21.9 us (93%)
  local copies, waits for them, and re-layouts  1.47 us (6%)
    pallas_call x1, Pallas kernels, on_device_fused(): pl.pallas_call(functools.partial(kernel, ns, ng, 1.0 / math.sqrt(rows * n...  21.9 us
    unnamed x1, local copies, waits for them, and re-layouts  1.47 us

profile of v2, /device:TPU:0, one launch (start us, length us, event | category | flops | bytes accessed | tf_op | source)
XLA Modules:
  0.0 23.4 jit_solution(17359444346158984762)
XLA Ops:
  0.0 21.9 %shard_map.46 = bf16[32,1024]{1,0:T(8,128)(2,1)} custom-call(s32[16]{0:T(128)} %bins_hbm.1, f32[1,4096]{1,0:T(1,128)} %bitcast.1, bf16[32,1024]{1,0:T(8,128)(2,1)} %hist_hbm.1, s32[32,4096]{1,0:T(8,128)} %delays_hbm.1), custom_call_target="tpu_custom_call" | custom-call | tf_op jit(solution)/shard_map/pallas_call | solution.py:373
  21.9 1.5 %copy.6 = bf16[32,1024]{1,0:T(8,128)(2,1)} copy(bf16[32,1024]{1,0:T(8,128)(2,1)} %shard_map.46) | data formatting | bytes 131072

commit v3 on v2

--- a/solution.py
+++ b/solution.py
@@ -162,7 +162,7 @@
     spec_in,
     part_out,
     part_in,
-    bar_out,
+    part_sum,
     bar_in,
     adj,
     local_sem,
@@ -185,7 +185,13 @@
     length = times * ng
 
     def sens_at(offset):
-        return lax.rem(sens + offset, ns)
+        if ns != 8:
+            return lax.rem(sens + offset, ns)
+        plane = lax.rem(sens // 4 + offset // 4, 2)
+        pair = lax.rem(sens // 2 + offset // 2, 2)
+        return 4 * plane + 2 * pair + lax.rem(sens + offset, 2)
+
+    order = list(range(ns - 1, 0, -1))
 
     def grp_at(offset):
         return lax.rem(grp + offset, ng)
@@ -272,17 +278,18 @@
     high = spread.astype(bf16).astype(f32)
     lhs = jnp.concatenate([high, spread - high], 0).astype(bf16)
 
-    def steered_part(owner):
-        at = pl.ds(pl.multiple_of(owner * width, width), width)
+    for owner in range(ns):
+        at = slice(owner * width, (owner + 1) * width)
         product = jnp.dot(lhs, steer[:, at], preferred_element_type=f32)
         product = product[0:8] + product[8:16]
-        return jnp.concatenate([product[:, 0:half], product[:, half:width]], 0)
+        product = jnp.concatenate([product[:, 0:half], product[:, half:width]], 0)
+        part_sum[owner] = product
+        part_out[owner] = product.astype(bf16)
 
     part_copies = []
-    for k in range(1, ns):
-        part_out[k - 1] = steered_part(sens_at(k)).astype(bf16)
+    for k in order:
         copy = pltpu.make_async_remote_copy(
-            src_ref=part_out.at[k - 1],
+            src_ref=part_out.at[sens_at(k)],
             dst_ref=part_in.at[k - 1],
             send_sem=part_send.at[k - 1],
             recv_sem=part_recv.at[k - 1],
@@ -291,24 +298,24 @@
         )
         copy.start()
         part_copies.append(copy)
-    total = steered_part(sens)
+    total = part_sum[sens]
     map_copy.wait()
     first = map_own[:, 0:half]
     second = map_own[:, half:width]
     weight = (2.0 * scale * scale) * jnp.concatenate(
         [jnp.broadcast_to(first, (8, half)), jnp.broadcast_to(second, (8, half))], 0
     )
+    for copy in part_copies:
+        copy.wait_recv()
     for k in range(1, ns):
-        part_copies[k - 1].wait_recv()
         total = total + part_in[k - 1].astype(f32)
-    bar = (weight * total).astype(bf16)
-    bar_out[...] = bar
+    bar_in[sens] = (weight * total).astype(bf16)
 
     bar_copies = []
-    for k in range(1, ns):
+    for k in order:
         copy = pltpu.make_async_remote_copy(
-            src_ref=bar_out,
-            dst_ref=bar_in.at[k - 1],
+            src_ref=bar_in.at[sens],
+            dst_ref=bar_in.at[sens],
             send_sem=bar_send.at[k - 1],
             recv_sem=bar_recv.at[k - 1],
             device_id={"sens": sens_at(k)},
@@ -317,24 +324,19 @@
         copy.start()
         bar_copies.append(copy)
 
-    def back_part(values, owner):
-        sides = []
+    for copy in bar_copies:
+        copy.wait_recv()
+    sides = [jnp.zeros((16, 256), f32)] * 2
+    for owner in range(ns):
         for side in range(2):
-            at = pl.ds(pl.multiple_of(owner * width + side * half, half), half)
-            sides.append(
-                lax.dot_general(
-                    values,
-                    steer[:, at],
-                    (((1,), (1,)), ((), ())),
-                    preferred_element_type=f32,
-                )
+            start = owner * width + side * half
+            sides[side] = sides[side] + lax.dot_general(
+                bar_in[owner],
+                steer[:, start : start + half],
+                (((1,), (1,)), ((), ())),
+                preferred_element_type=f32,
             )
-        return sides[0][0:8] + sides[1][8:16]
-
-    back = back_part(bar, sens)
-    for k in range(1, ns):
-        bar_copies[k - 1].wait_recv()
-        back = back + back_part(bar_in[k - 1], sens_at(ns - k))
+    back = sides[0][0:8] + sides[1][8:16]
     back = jnp.where(own_block, back, 0.0)
     back = back[:, 0:128] + back[:, 128:256]
     back = back + pltpu.roll(back, 64, 1)
@@ -389,10 +391,10 @@
             vmem((256, points), jnp.bfloat16),
             vmem((ng, 8, 128), jnp.float32),
             vmem((ng - 1, 8, 128), jnp.float32),
+            vmem((ns, 16, half), jnp.bfloat16),
             vmem((ns - 1, 16, half), jnp.bfloat16),
-            vmem((ns - 1, 16, half), jnp.bfloat16),
-            vmem((16, half), jnp.bfloat16),
-            vmem((ns - 1, 16, half), jnp.bfloat16),
+            vmem((ns, 16, half), jnp.float32),
+            vmem((ns, 16, half), jnp.bfloat16),
             vmem((ng, 16, 128), jnp.bfloat16),
             dma((4,)),
             dma((ng - 1,)),

time: 23.6 us -> 23.2 us (0.983)
  Pallas kernels: 21.9 us -> 21.5 us
    pallas_call x1, Pallas kernels: 21.9 us -> 21.5 us  [on_device_fused(): pl.pallas_call(functools.partial(kernel, ns, ng, 1.0 / math.sqrt(rows * n...]
where the time goes in v3:
time: 23.2 us; the launch traced here: 23 us
  Pallas kernels  21.5 us (93%)
  local copies, waits for them, and re-layouts  1.47 us (6%)
    pallas_call x1, Pallas kernels, on_device_fused(): pl.pallas_call(functools.partial(kernel, ns, ng, 1.0 / math.sqrt(rows * n...  21.5 us
    unnamed x1, local copies, waits for them, and re-layouts  1.47 us

profile of v3, /device:TPU:0, one launch (start us, length us, event | category | flops | bytes accessed | tf_op | source)
XLA Modules:
  0.0 23.0 jit_solution(9830123205072468907)
XLA Ops:
  0.0 21.5 %shard_map.46 = bf16[32,1024]{1,0:T(8,128)(2,1)} custom-call(s32[16]{0:T(128)} %bins_hbm.1, f32[1,4096]{1,0:T(1,128)} %bitcast.1, bf16[32,1024]{1,0:T(8,128)(2,1)} %hist_hbm.1, s32[32,4096]{1,0:T(8,128)} %delays_hbm.1), custom_call_target="tpu_custom_call" | custom-call | tf_op jit(solution)/shard_map/pallas_call | solution.py:375
  21.5 1.5 %copy.6 = bf16[32,1024]{1,0:T(8,128)(2,1)} copy(bf16[32,1024]{1,0:T(8,128)(2,1)} %shard_map.46) | data formatting | bytes 131072
